TPU v7x, 512 devices: a whole 4x8x8 slice. The times are simulated.
512 devices in a mesh: ctx: 32 (over x_hi, y, core), head: 16 (over x_lo, z).
Axes of the slice: x: 4 (x_hi: 2, x_lo: 2; x = x_hi * 2 + x_lo), y: 8, z: 8, core: 2. Of those that a mesh axis runs over, the one named last changes fastest.
Arguments:
- query: bfloat16 [4096, 4096], P('ctx', 'head'), may hold values from -5 to 5
- key: bfloat16 [4096, 4096], P('ctx', 'head'), may hold values from -5 to 5
- value: bfloat16 [4096, 4096], P('ctx', 'head'), may hold values from -6 to 6
- query_tangent: bfloat16 [4096, 4096], P('ctx', 'head'), may hold values from -6 to 6
- key_tangent: bfloat16 [4096, 4096], P('ctx', 'head'), may hold values from -6 to 6
- value_tangent: bfloat16 [4096, 4096], P('ctx', 'head'), may hold values from -6 to 6
- out_weight: bfloat16 [4096, 4096], P('head'), may hold values from -0.09375 to 0.09375
- block_mask: int32 [32, 32], replicated, may hold values from 0 to 1, as said below
- probe: int32 [4096, 4096], P(('ctx', 'head')), may hold values 0 or 1
Outputs:
- output: bfloat16 [4096, 4096], P(('ctx', 'head'))
- output_tangent: bfloat16 [4096, 4096], P(('ctx', 'head'))
- trace_terms: float32 [4096], P(('ctx', 'head'))
Inputs may be any that keep to these rules, and one draw needn't show every extreme that they name: `block_mask`: entry (b, b) is 1 for every block b.
All inputs are finite; a program needn't handle non-finite values. No bound on the sum of `probe` on one device may be relied on, other than what follows from the above.
Results may differ from a plain program's by a relative error of at most 0.005.
Values may be sent and summed in bfloat16 or wider, within the bound.
A program may use at most 64 MiB of HBM per device.

v0:
```python
import math

import jax
import jax.numpy as jnp
from jax import lax
from jax.sharding import PartitionSpec as P

HD = 128
BLOCK = 128


floor_score = -1e30


def on_device(
    query, key, value, query_tangent, key_tangent, value_tangent, out_weight, block_mask, probe
):
    row_count = query.shape[0]
    local_heads = query.shape[1] // HD
    score_scale = 1.0 / math.sqrt(HD)
    block_count = block_mask.shape[1]
    highest = lax.Precision.HIGHEST
    query_main = query.reshape(row_count, local_heads, HD)
    query_dot = query_tangent.reshape(row_count, local_heads, HD)
    ctx_index = lax.axis_index("ctx")
    mask_rows = lax.dynamic_slice_in_dim(
        block_mask, ctx_index * (row_count // BLOCK), row_count // BLOCK, 0
    )

    def update(state, key_tile, value_tile, key_dtile, value_dtile, allowed):
        run_max, run_total, run_bend, acc_out, acc_tan = state
        key_width = key_tile.shape[0]
        key_r = key_tile.reshape(key_width, local_heads, HD)
        key_dr = key_dtile.reshape(key_width, local_heads, HD)
        value_r = value_tile.astype(jnp.float32).reshape(key_width, local_heads, HD)
        value_dr = value_dtile.astype(jnp.float32).reshape(key_width, local_heads, HD)
        scores = (
            jnp.einsum("qhd,khd->hqk", query_main, key_r, preferred_element_type=jnp.float32)
            * score_scale
        )
        slopes = (
            jnp.einsum("qhd,khd->hqk", query_dot, key_r, preferred_element_type=jnp.float32)
            + jnp.einsum("qhd,khd->hqk", query_main, key_dr, preferred_element_type=jnp.float32)
        ) * score_scale
        allowed_h = allowed[None, :, :]
        new_max = jnp.maximum(run_max, jnp.max(jnp.where(allowed_h, scores, floor_score), axis=-1))
        rescale = jnp.exp(run_max - new_max)
        weights = jnp.where(allowed_h, jnp.exp(scores - new_max[..., None]), 0.0)
        tilted = weights * slopes
        new_total = run_total * rescale + jnp.sum(weights, axis=-1)
        new_bend = run_bend * rescale + jnp.sum(tilted, axis=-1)
        factor = rescale.T[:, :, None]
        new_out = acc_out * factor + jnp.einsum("hqk,khd->qhd", weights, value_r, precision=highest)
        new_tan = (
            acc_tan * factor
            + jnp.einsum("hqk,khd->qhd", weights, value_dr, precision=highest)
            + jnp.einsum("hqk,khd->qhd", tilted, value_r, precision=highest)
        )
        return (new_max, new_total, new_bend, new_out, new_tan)

    def add_tile(state, key_tile, value_tile, key_dtile, value_dtile, key_first):
        key_width = key_tile.shape[0]
        col_block = (key_first + jnp.arange(key_width, dtype=jnp.int32)) // BLOCK
        column_pick = (
            col_block[None, :] == jnp.arange(block_count, dtype=jnp.int32)[:, None]
        ).astype(jnp.int32)
        block_tile = jnp.dot(mask_rows, column_pick)
        allowed = jnp.repeat(block_tile, BLOCK, axis=0) > 0
        return update(state, key_tile, value_tile, key_dtile, value_dtile, allowed)

    start_state = (
        jnp.full((local_heads, row_count), floor_score, jnp.float32),
        jnp.zeros((local_heads, row_count), jnp.float32),
        jnp.zeros((local_heads, row_count), jnp.float32),
        jnp.zeros((row_count, local_heads, HD), jnp.float32),
        jnp.zeros((row_count, local_heads, HD), jnp.float32),
    )
    keys_p = lax.all_gather(key, "ctx", axis=0, tiled=True)
    values_p = lax.all_gather(value, "ctx", axis=0, tiled=True)
    keys_dp = lax.all_gather(key_tangent, "ctx", axis=0, tiled=True)
    values_dp = lax.all_gather(value_tangent, "ctx", axis=0, tiled=True)
    key_total = keys_p.shape[0]
    key_width = math.gcd(key_total, 512)
    turn_count = key_total // key_width

    def one_turn(turn_at, carried):
        key_first = turn_at * key_width
        return add_tile(
            carried,
            lax.dynamic_slice_in_dim(keys_p, key_first, key_width, 0),
            lax.dynamic_slice_in_dim(values_p, key_first, key_width, 0),
            lax.dynamic_slice_in_dim(keys_dp, key_first, key_width, 0),
            lax.dynamic_slice_in_dim(values_dp, key_first, key_width, 0),
            key_first,
        )

    run_max, run_total, run_bend, acc_out, acc_tan = lax.fori_loop(
        0, turn_count, one_turn, start_state
    )
    total_q = run_total.T[:, :, None]
    attended_f = acc_out / total_q
    attended_df = acc_tan / total_q - run_bend.T[:, :, None] / total_q * attended_f
    attended = attended_f.reshape(row_count, local_heads * HD).astype(jnp.bfloat16)
    attended_dot = attended_df.reshape(row_count, local_heads * HD).astype(jnp.bfloat16)
    projected = lax.psum_scatter(
        jnp.concatenate(
            [
                jnp.dot(attended, out_weight, preferred_element_type=jnp.float32),
                jnp.dot(attended_dot, out_weight, preferred_element_type=jnp.float32),
            ],
            axis=1,
        ),
        "head",
        scatter_dimension=0,
        tiled=True,
    )
    model_width = out_weight.shape[1]
    output_main = projected[:, :model_width]
    output_dot = projected[:, model_width:]
    probe_sign = (2 * probe - 1).astype(jnp.float32)
    trace_terms = jnp.sum(probe_sign * output_dot, axis=1) / math.sqrt(model_width)
    return (output_main.astype(jnp.bfloat16), output_dot.astype(jnp.bfloat16), trace_terms)


def solution(mesh):
    placed = (
        P("ctx", "head"),
        P("ctx", "head"),
        P("ctx", "head"),
        P("ctx", "head"),
        P("ctx", "head"),
        P("ctx", "head"),
        P("head", None),
        P(),
        P(("ctx", "head"), None),
    )
    return jax.shard_map(
        on_device,
        mesh=mesh,
        in_specs=placed,
        out_specs=(P(("ctx", "head"), None), P(("ctx", "head"), None), P(("ctx", "head"))),
        check_vma=False,
    )
```

profile of v0, /device:TPU:8, one launch (start us, length us, event | category | flops | bytes accessed | tf_op | source)
XLA Modules:
  0.0 500.1 jit_solution(2329391193164328483)
XLA Ops:
  7.2 1.7 copy.19
  9.0 1.6 copy.22
  10.7 1.6 copy.23
  12.3 1.6 copy.24
  16.2 1.3 constant_dynamic-slice_fusion.4
  17.5 81.0 %all-gather.5.cloned.1.call-done = bf16[4096,256]{0,1:T(8,128)(2,1)} async-done(((bf16[128,256]{0,1:T(8,128)(2,1)}), bf16[4096,256]{0,1:T(8,128)(2,1)}) %all-gather.5.cloned.1.call-update) | async-done | bytes 2097168 | tf_op jit(solution)/shard_map/all_gather | solution.py:78
  98.5 82.6 %all-gather.7.cloned.1.call-done = bf16[4096,256]{0,1:T(8,128)(2,1)} async-done(((bf16[128,256]{0,1:T(8,128)(2,1)}), bf16[4096,256]{0,1:T(8,128)(2,1)}) %all-gather.7.cloned.1.call-update) | async-done | bytes 2097168 | tf_op jit(solution)/shard_map/all_gather | solution.py:80
  181.1 82.1 %all-gather.9.cloned.1.call-done = bf16[4096,256]{0,1:T(8,128)(2,1)} async-done(((bf16[128,256]{0,1:T(8,128)(2,1)}), bf16[4096,256]{0,1:T(8,128)(2,1)}) %all-gather.9.cloned.1.call-update) | async-done | bytes 2097168 | tf_op jit(solution)/shard_map/all_gather | solution.py:79
  263.2 81.9 %all-gather.11.cloned.1.call-done = bf16[4096,256]{0,1:T(8,128)(2,1)} async-done(((bf16[128,256]{0,1:T(8,128)(2,1)}), bf16[4096,256]{0,1:T(8,128)(2,1)}) %all-gather.11.cloned.1.call-update) | async-done | bytes 2097168 | tf_op jit(solution)/shard_map/all_gather | solution.py:81
  345.1 59.7 %while.24 = (s32[]{:T(128)}, f32[2,128]{1,0:T(2,128)S(1)}, f32[2,128]{1,0:T(2,128)S(1)}, f32[2,128]{1,0:T(2,128)}, f32[128,2,128]{0,2,1:T(8,128)}, /*index=5*/f3...) while((s32[]{:T(128)}, f32[2,128]{1,0:T(2,128)S(1)}, ...), condition=%wide.region_4.5_spmd.clone, body=%wide.region_0.4_spmd.clone.sunk | while | flops 707029504 | bytes 10979776 | solution.py:97
  345.1 1.1 constant_dynamic-slice_fusion.7
  348.7 1.1 constant_dynamic-slice_fusion.8
  352.0 1.1 constant_dynamic-slice_fusion.7
  355.0 1.2 fusion.71
  356.2 1.1 constant_dynamic-slice_fusion.8
  359.5 1.1 constant_dynamic-slice_fusion.7
  362.6 1.2 fusion.71
  363.7 1.1 constant_dynamic-slice_fusion.8
  367.1 1.1 constant_dynamic-slice_fusion.7
  370.1 1.2 fusion.71
  371.3 1.1 constant_dynamic-slice_fusion.8
  374.6 1.1 constant_dynamic-slice_fusion.7
  377.6 1.2 fusion.71
  382.2 1.1 constant_dynamic-slice_fusion.7
  385.2 1.2 fusion.71
  389.7 1.1 constant_dynamic-slice_fusion.7
  392.7 1.2 fusion.71
  397.2 1.1 constant_dynamic-slice_fusion.7
  400.3 1.2 fusion.71
  407.4 2.3 pad_maximum_fusion
  409.7 80.7 %reduce-scatter.2.cloned.1.call-done = f32[8,8192]{1,0:T(8,128)} async-done(((f32[128,8192]{1,0:T(8,128)}), f32[8,8192]{1,0:T(8,128)}) %reduce-scatter.2.cloned.1.call-update) | async-done | bytes 262160 | tf_op jit(solution)/shard_map/reduce_scatter | solution.py:105
  492.0 1.6 fusion.19
  (178 shorter events, 44.5 us)
Async XLA Ops:
  7.2 399.2 %copy-start = (bf16[256,4096]{1,0:T(8,128)(2,1)S(1)}, bf16[256,4096]{1,0:T(8,128)(2,1)}, u32[]{:S(2)}) copy-start(bf16[256,4096]{1,0:T(8,128)(2,1)} %param.17) | copy-start | bytes 6291460
  7.2 91.3 %all-gather.5.cloned.1.call-start = ((), (), s32[]{:S(2)}) async-start(), calls=%async_computation.1 | async-start | bytes 2162688 | tf_op jit(solution)/shard_map/all_gather | solution.py:78
  9.0 172.1 %all-gather.7.cloned.1.call-start = ((), (), s32[]{:S(2)}) async-start(), calls=%async_computation.2 | async-start | bytes 2162688 | tf_op jit(solution)/shard_map/all_gather | solution.py:80
  10.6 252.6 %all-gather.9.cloned.1.call-start = ((), (), s32[]{:S(2)}) async-start(), calls=%async_computation.3 | async-start | bytes 2162688 | tf_op jit(solution)/shard_map/all_gather | solution.py:79
  12.3 332.8 %all-gather.11.cloned.1.call-start = ((), (), s32[]{:S(2)}) async-start(), calls=%async_computation.4 | async-start | bytes 2162688 | tf_op jit(solution)/shard_map/all_gather | solution.py:81
  13.9 476.5 %reduce-scatter.2.cloned.1.call-start = ((), (), s32[]{:S(2)}) async-start(), calls=%async_computation.5 | async-start | bytes 4456448 | tf_op jit(solution)/shard_map/reduce_scatter | solution.py:105
  347.6 2.1 copy-start.1
  347.6 2.7 copy-start.3
  350.3 1.7 copy-start.2
  354.5 2.7 copy-start.1
  354.6 3.3 copy-start.3
  357.9 1.7 copy-start.2
  362.1 2.7 copy-start.1
  362.1 3.3 copy-start.3
  365.4 1.7 copy-start.2
  369.6 2.7 copy-start.1
  369.6 3.3 copy-start.3
  372.9 1.7 copy-start.2
  377.1 2.7 copy-start.1
  377.2 3.3 copy-start.3
  380.5 1.7 copy-start.2
  384.7 2.7 copy-start.1
  384.7 3.3 copy-start.3
  388.0 1.7 copy-start.2
  392.2 2.7 copy-start.1
  392.2 3.3 copy-start.3
  395.6 1.7 copy-start.2
  399.8 2.7 copy-start.1
  399.8 3.3 copy-start.3
  403.1 1.7 copy-start.2
  409.7 80.7 %copy-start.4 = (s32[8,4096]{1,0:T(8,128)S(1)}, s32[8,4096]{1,0:T(8,128)}, u32[]{:S(2)}) copy-start(s32[8,4096]{1,0:T(8,128)} %param.19) | copy-start | bytes 393220
Sparse Core Ops, SparseCore 0:
  11.7 86.6 all-gather.4
  102.2 78.8 all-gather.6
  184.2 78.8 all-gather.8
  266.2 78.8 all-gather.10
  409.8 80.5 reduce-scatter.1
where the time goes:
time: 501 us; the launch traced here: 500 us
  waiting for transfers between devices  408 us (81%)
  matrix products  32.5 us (6%)
  local copies, waits for them, and re-layouts  28.7 us (6%)
  other arithmetic  15.6 us (3%)
  between operations  13.9 us (3%)
    all_gather x1, waiting for transfers between devices, on_device(): keys_dp = lax.all_gather(key_tangent, 'ctx', axis=0, tiled=True)  82.6 us
    all_gather x1, waiting for transfers between devices, on_device(): values_p = lax.all_gather(value, 'ctx', axis=0, tiled=True)  82.1 us
    all_gather x1, waiting for transfers between devices, on_device(): values_dp = lax.all_gather(value_tangent, 'ctx', axis=0, tiled=True)  81.9 us
    all_gather x1, waiting for transfers between devices, on_device(): keys_p = lax.all_gather(key, 'ctx', axis=0, tiled=True)  81 us
    reduce_scatter x1, waiting for transfers between devices, on_device(): lax.psum_scatter(jnp.concatenate([jnp.dot(attended, out_weight, preferred...  80.7 us
  transfers between devices with their start and end apart: 5, of which 5 were waited for; matrix products, arithmetic and copies ran while one was open for 2% of the time, Pallas kernels for 0%

commit v1 on v0

v1 whole, which is shorter than its diff:
```python
import functools
import math

import jax
import jax.numpy as jnp
from jax import lax
from jax.experimental import pallas as pl
from jax.experimental.pallas import tpu as pltpu
from jax.sharding import PartitionSpec as P

HD = 128
BLOCK = 128
RING = 8
PAIR = 2 * BLOCK
MASKED = -1e30
FLOWS = 4
SCALE = 1.0 / math.sqrt(HD)
SCALE2 = SCALE * math.log2(math.e)


def dot(a, b):
    return jnp.dot(a, b, preferred_element_type=jnp.float32)


def dot_t(a, b):
    return lax.dot_general(a, b, (((1,), (1,)), ((), ())), preferred_element_type=jnp.float32)


def kernel(
    query, key, value, query_t, key_t, value_t, weight, mask, probe,
    out_main, out_tan, out_trace,
    shards, queries, peak, acc_v, acc_t, sums, att, att_in, w_buf, probe_buf, part,
    z_out, z_in, x_out, x_in,
    swap_send, swap_recv, local_sem, load_sem, ring_send, ring_recv, share_send, share_recv,
    att_send, att_recv, w_send, w_recv, z_send, z_recv, x_send, x_recv,
):
    ctx = lax.axis_index("ctx")
    head = lax.axis_index("head")
    core, chip = ctx % 2, ctx // 2
    y, half = chip % RING, chip // RING
    z, xlo = head % RING, head // RING
    far = 1 - half
    width = weight.shape[1]
    wide = width // 2
    cols = wide // FLOWS

    sibling = {"ctx": chip * 2 + 1 - core, "head": head}
    opposite = {"ctx": (far * RING + y) * 2 + core, "head": head}
    y_next = [
        {"ctx": (half * RING + (y + step) % RING) * 2 + core, "head": head}
        for step in (1, RING - 1)
    ]
    z_next = [{"ctx": ctx, "head": xlo * RING + (z + step) % RING} for step in (1, RING - 1)]
    x_next = {"ctx": ctx, "head": (1 - xlo) * RING + z}
    fourth = {"ctx": (far * RING + y) * 2 + core, "head": (1 - xlo) * RING + z}

    mine = pl.ds(pl.multiple_of(half * HD, HD), HD)
    theirs = pl.ds(pl.multiple_of(far * HD, HD), HD)
    left, right = pl.ds(0, HD), pl.ds(HD, HD)

    def places(which):
        at = which * RING + y
        rows = pl.ds(pl.multiple_of(which * BLOCK, BLOCK), BLOCK)
        return [
            (key, shards.at[at, core, 0, :, left]),
            (key_t, shards.at[at, core, 0, :, right]),
            (value, shards.at[at, core, 1, :, left]),
            (value_t, shards.at[at, core, 1, :, right]),
            (query_t, queries.at[rows, left]),
            (query, queries.at[rows, right]),
        ]

    local = [
        pltpu.make_async_copy(src.at[:, mine], dst, local_sem.at[i])
        for i, (src, dst) in enumerate(places(half))
    ]
    for copy in local:
        copy.start()

    barrier = pltpu.get_barrier_semaphore()
    partners = [sibling, opposite] + y_next + z_next + [x_next, fourth]
    for partner in partners:
        pl.semaphore_signal(barrier, inc=1, device_id=partner, device_id_type=pl.DeviceIdType.MESH)
    pl.semaphore_wait(barrier, len(partners))

    def remote(src, dst, send, recv, device):
        return pltpu.make_async_remote_copy(
            src_ref=src, dst_ref=dst, send_sem=send, recv_sem=recv,
            device_id=device, device_id_type=pl.DeviceIdType.MESH,
        )

    def place(h, hop):
        which = half if h == 0 else far
        return which * RING + (y + hop + RING) % RING

    def message(d, h, k, e, arriving=False):
        sign = 1 if d == 0 else -1
        slot = place(h, -sign * (k + 1) if arriving else -sign * k)
        ref = shards.at[slot, core, e]
        return remote(ref, ref, ring_send.at[d, h, k, e], ring_recv.at[d, h, k, e], y_next[d])

    def share(h, hop, arriving=False):
        ref = shards.at[place(h, hop), 1 - core if arriving else core]
        return remote(ref, ref, share_send.at[h, hop % RING], share_recv.at[h, hop % RING], sibling)

    crossing = [
        remote(src.at[:, theirs], dst, swap_send.at[i], swap_recv.at[i], opposite)
        for i, (src, dst) in enumerate(places(half))
    ]
    landing = [
        remote(src.at[:, theirs], dst, swap_send.at[i], swap_recv.at[i], opposite)
        for i, (src, dst) in enumerate(places(far))
    ]
    for copy in crossing[:4]:
        copy.start()
    for e in range(2):
        for copy in local[2 * e : 2 * e + 2]:
            copy.wait()
        for d in range(2):
            message(d, 0, 0, e).start()
    share(0, 0).start()

    my_cols = pl.ds(pl.multiple_of(xlo * wide, wide), wide)
    its_cols = pl.ds(pl.multiple_of((1 - xlo) * wide, wide), wide)
    loads = [
        pltpu.make_async_copy(weight.at[at, my_cols], w_buf.at[i], load_sem.at[i])
        for i, at in enumerate([mine, theirs])
    ] + [pltpu.make_async_copy(probe, probe_buf, load_sem.at[2])]
    for copy in loads:
        copy.start()
    turn = (core + half) % 2
    w_fetch = remote(
        weight.at[pl.ds(pl.multiple_of(core * HD, HD), HD), its_cols], w_buf.at[2 + turn],
        w_send.at[0], w_recv.at[0], x_next,
    )

    def w_share(arriving=False):
        ref = w_buf.at[2 + (1 - turn if arriving else turn)]
        return remote(ref, ref, w_send.at[1], w_recv.at[1], sibling)

    peak[...] = jnp.full(peak.shape, MASKED, jnp.float32)
    sums[...] = jnp.zeros(sums.shape, jnp.float32)
    acc_v[...] = jnp.zeros(acc_v.shape, jnp.float32)
    acc_t[...] = jnp.zeros(acc_t.shape, jnp.float32)
    for copy in local[4:]:
        copy.wait()

    def split(x):
        high = x.astype(jnp.bfloat16)
        return high, (x - high.astype(jnp.float32)).astype(jnp.bfloat16)

    def attend(slot, blocks=(0, 1)):
        keys = jnp.concatenate([shards[slot, 0, 0], shards[slot, 1, 0]], axis=0)
        values = jnp.concatenate([shards[slot, 0, 1], shards[slot, 1, 1]], axis=0)
        ones = jnp.ones((PAIR, HD), jnp.bfloat16)
        value_one = jnp.concatenate([values[:, :HD], ones], axis=1)
        for r in blocks:
            at = pl.ds(pl.multiple_of(r * BLOCK, BLOCK), BLOCK)
            scores = dot_t(queries[at, HD:], keys[:, :HD]) * SCALE2
            slopes = dot_t(queries[at, :], keys)
            bias = [
                jnp.where(mask[(r * RING + y) * 2 + core, slot * 2 + b] == 1, 0.0, MASKED).astype(jnp.float32)
                for b in range(2)
            ]
            scores = jnp.concatenate(
                [scores[:, :BLOCK] + bias[0], scores[:, BLOCK:] + bias[1]], axis=1
            )
            old = peak[at, :]
            new = jnp.maximum(old, jnp.max(scores, axis=1, keepdims=True))
            fade = jnp.exp2(old - new)
            weights = jnp.exp2(scores - jnp.concatenate([new, new], axis=1))
            w_high, w_low = split(weights)
            t_high, t_low = split(weights * slopes)
            fade2 = jnp.concatenate([fade, fade], axis=1)
            peak[at, :] = new
            sums[at, :] = sums[at, :] * fade + jnp.sum(weights, axis=1, keepdims=True)
            acc_v[at, :] = acc_v[at, :] * fade2 + (dot(w_high, values) + dot(w_low, values))
            acc_t[at, :] = acc_t[at, :] * fade2 + (dot(t_high, value_one) + dot(t_low, value_one))

    def ring(h, k, e):
        for d in range(2):
            message(d, h, k, e, True).wait_recv()
            if k < 2 or e == d:
                message(d, h, k + 1, e).start()
        if e == 1:
            share(h, -k - 1).start()
            share(h, k + 1).start()

    def last(h):
        for d in range(2):
            message(d, h, 3, d, True).wait_recv()
        share(h, 4).start()

    def cross(e):
        for copy in landing[2 * e : 2 * e + 2]:
            copy.wait_recv()
        for d in range(2):
            message(d, 1, 0, e).start()
        if e == 1:
            share(1, 0).start()
            w_fetch.start()

    def send_rows():
        for copy in crossing[4:]:
            copy.start()

    def rows_of_opposite():
        for copy in landing[4:]:
            copy.wait_recv()

    def share_weight():
        w_fetch.wait_recv()
        w_share().start()

    do = functools.partial
    steps = [
        ([do(ring, 0, 0, 0), send_rows, do(ring, 0, 0, 1), do(cross, 0), do(cross, 1), rows_of_opposite], (0, 0)),
        ([do(ring, 0, 1, 0)], (1, 0)),
        ([do(ring, 0, 1, 1)], (0, -1)),
        ([do(ring, 1, 0, 0)], (0, 1)),
        ([do(ring, 1, 0, 1)], (0, -2)),
        ([do(ring, 0, 2, 0)], (0, 2)),
        ([do(ring, 0, 2, 1)], (1, -1)),
        ([do(ring, 1, 1, 0)], (1, 1)),
        ([do(ring, 1, 1, 1)], (0, -3)),
        ([do(last, 0)], (0, 3)),
        ([share_weight], (1, -2)),
        ([do(ring, 1, 2, 0)], (1, 2)),
        ([do(ring, 1, 2, 1)], (0, 4)),
        ([], (1, -3)),
        ([], (1, 3)),
        ([do(last, 1)], (1, 4)),
    ]

    def step(n, carry):
        slot = 0
        for i, (actions, here) in enumerate(steps):
            if i == len(steps) - 1:
                break
            slot = slot + jnp.where(n == i, place(*here), 0)

            @pl.when(n == i)
            def _(actions=actions, here=here):
                for action in actions:
                    action()
                share(*here, True).wait_recv()

        attend(slot)
        return carry

    lax.fori_loop(0, len(steps) - 1, step, 0)

    hand_back = [
        remote(att.at[which], att_in.at[i], att_send.at[i], att_recv.at[i], device)
        for i, (which, device) in enumerate([(far, opposite), (half, x_next), (far, fourth)])
    ]

    def attended(b):
        at = pl.ds(pl.multiple_of(b * BLOCK, BLOCK), BLOCK)
        total = sums[at, :]
        main = acc_v[at, :HD] / total
        tangent = (acc_v[at, HD:] + acc_t[at, :HD] * SCALE) / total - (
            acc_t[at, HD:] * SCALE
        ) / total * main
        pieces = []
        for zz in range(RING):
            for xx in range(2):
                first = (xx * RING + zz) * 8
                pieces += [main[first : first + 8], tangent[first : first + 8]]
        att[b] = jnp.concatenate(pieces, axis=0).astype(jnp.bfloat16)

    actions, here = steps[-1]
    for action in actions:
        action()
    share(*here, True).wait_recv()
    attend(place(*here), (far,))
    attended(far)
    hand_back[0].start()
    hand_back[2].start()
    attend(place(*here), (half,))
    attended(half)
    hand_back[1].start()

    for h in range(2):
        for d in range(2):
            for k in range(3):
                for e in range(2):
                    message(d, h, k, e).wait_send()
            message(d, h, 3, d).wait_send()
        for hop in range(-3, 5):
            share(h, hop).wait_send()
    for copy in crossing:
        copy.wait_send()
    for copy in loads:
        copy.wait()
    w_fetch.wait_send()
    w_share().wait_send()
    w_share(True).wait_recv()

    def project(f, begin):
        at = slice(f * cols, (f + 1) * cols)
        rows_in = [att[half], att_in[1]] if begin else [att_in[0], att_in[2]]
        lhs = jnp.concatenate(rows_in, axis=1)
        heads = (0, 2) if begin else (1, 3)
        term = dot(lhs, jnp.concatenate([w_buf[i, :, at] for i in heads], axis=0))
        part[:, at] = term if begin else part[:, at] + term

    chunk = 32

    def z_message(d, f, s):
        rows = pl.ds(0, chunk if s < 3 else chunk + 16)
        return remote(
            z_out.at[d, f, s, rows], z_in.at[d, f, s, rows], z_send.at[d, f, s], z_recv.at[d, f, s],
            z_next[d],
        )

    def send_sum(d, f, s, has_input):
        sign = 1 if d == 0 else -1
        target = (z + sign * (4 - s) + RING) % RING
        if has_input:
            z_message(d, f, s - 1).wait_recv()
        summed = part[
            pl.ds(pl.multiple_of(target * chunk, chunk), chunk), f * cols : (f + 1) * cols
        ]
        if has_input:
            summed = summed + z_in[d, f, s - 1, :chunk, :].astype(jnp.float32)
        high, low = split(summed)
        z_out[d, f, s, :chunk, :] = high
        if s == 3:
            low = low.astype(jnp.float32)
            z_out[d, f, s, chunk:, :] = jnp.concatenate([low[8:16], low[24:]], axis=0).astype(
                jnp.bfloat16
            )
        z_message(d, f, s).start()

    def far_side(f):
        return 1 if f < FLOWS // 2 else 0

    order = [f + side for f in range(FLOWS // 2) for side in (0, FLOWS // 2)]
    hand_back[1].wait()
    for f in order:
        project(f, True)
    hand_back[0].wait()
    hand_back[2].wait()
    for f in order:
        project(f, False)
        send_sum(far_side(f), f, 0, False)
        send_sum(1 - far_side(f), f, 1, False)
    for s in (1, 2, 3):
        for f in order:
            send_sum(far_side(f), f, s, True)
            if s < 3:
                send_sum(1 - far_side(f), f, s + 1, True)

    def x_message(f):
        return remote(x_out.at[f], x_in.at[f], x_send.at[f], x_recv.at[f], x_next)

    def settle(f, which):
        own = pl.ds(pl.multiple_of(which * 16, 16), 16)
        at = slice(f * cols, (f + 1) * cols)
        low = z_in[0, f, 3, chunk:, :].astype(jnp.float32) + z_in[1, f, 3, chunk:, :].astype(jnp.float32)
        low = jnp.where(which == 0, low[:8], low[8:])
        return (
            part[pl.ds(pl.multiple_of(z * chunk + which * 16, 16), 16), at]
            + z_in[0, f, 3, own, :].astype(jnp.float32)
            + z_in[1, f, 3, own, :].astype(jnp.float32)
            + jnp.concatenate([jnp.zeros_like(low), low], axis=0)
        )

    for f in order:
        for d in range(2):
            z_message(d, f, 3).wait_recv()
        high, low = split(settle(f, 1 - xlo))
        low = low.astype(jnp.float32)[8:]
        x_out[f, :16, :] = high
        x_out[f, 16:, :] = jnp.concatenate([low, jnp.zeros_like(low)], axis=0).astype(jnp.bfloat16)
        x_message(f).start()

    def finish(main, tangent, side, f, trace):
        at = pl.ds(pl.multiple_of(side * wide + f * cols, cols), cols)
        out_main[:, at] = main.astype(jnp.bfloat16)
        out_tan[:, at] = tangent.astype(jnp.bfloat16)
        signed = (2 * probe_buf[:, at] - 1).astype(jnp.float32) * tangent
        for i in range(cols // HD):
            trace = trace + signed[:, i * HD : (i + 1) * HD]
        return trace

    trace = jnp.zeros((8, HD), jnp.float32)
    for f in order:
        final = settle(f, xlo)
        trace = finish(final[:8], final[8:], xlo, f, trace)
    for f in order:
        x_message(f).wait_recv()
        final = x_in[f].astype(jnp.float32)
        trace = finish(final[:8], final[8:16] + final[16:24], 1 - xlo, f, trace)
    at_row = lax.broadcasted_iota(jnp.int32, (8, HD), 0) == lax.broadcasted_iota(jnp.int32, (8, HD), 1)
    sums_of = jnp.broadcast_to(jnp.sum(trace, axis=1, keepdims=True) / math.sqrt(width), (8, HD))
    out_trace[...] = jnp.sum(jnp.where(at_row, sums_of, 0.0), axis=0, keepdims=True)[:, :8]

    for d in range(2):
        for f in range(FLOWS):
            for s in range(0 if d == far_side(f) else 1, 4):
                z_message(d, f, s).wait_send()
    for f in range(FLOWS):
        x_message(f).wait_send()


def on_device(
    query, key, value, query_tangent, key_tangent, value_tangent, out_weight, block_mask, probe
):
    width = out_weight.shape[1]
    wide = width // 2
    cols = wide // FLOWS
    anywhere = pl.BlockSpec(memory_space=pl.ANY)
    in_vmem = pl.BlockSpec(memory_space=pltpu.VMEM)
    bf16, f32 = jnp.bfloat16, jnp.float32
    dma = pltpu.SemaphoreType.DMA
    main, tangent, trace = pl.pallas_call(
        kernel,
        out_shape=(
            jax.ShapeDtypeStruct((8, width), bf16),
            jax.ShapeDtypeStruct((8, width), bf16),
            jax.ShapeDtypeStruct((1, 8), f32),
        ),
        in_specs=[anywhere] * 7 + [pl.BlockSpec(memory_space=pltpu.SMEM), anywhere],
        out_specs=(in_vmem, in_vmem, in_vmem),
        scratch_shapes=[
            pltpu.VMEM((2 * RING, 2, 2, BLOCK, PAIR), bf16),
            pltpu.VMEM((PAIR, PAIR), bf16),
            pltpu.VMEM((PAIR, HD), f32),
            pltpu.VMEM((PAIR, PAIR), f32),
            pltpu.VMEM((PAIR, PAIR), f32),
            pltpu.VMEM((PAIR, HD), f32),
            pltpu.VMEM((2, PAIR, HD), bf16),
            pltpu.VMEM((3, PAIR, HD), bf16),
            pltpu.VMEM((4, HD, wide), bf16),
            pltpu.VMEM((8, width), jnp.int32),
            pltpu.VMEM((PAIR, wide), f32),
            pltpu.VMEM((2, FLOWS, 4, 48, cols), bf16),
            pltpu.VMEM((2, FLOWS, 4, 48, cols), bf16),
            pltpu.VMEM((FLOWS, 32, cols), bf16),
            pltpu.VMEM((FLOWS, 32, cols), bf16),
            dma((6,)), dma((6,)), dma((6,)), dma((3,)),
            dma((2, 2, 4, 2)), dma((2, 2, 4, 2)), dma((2, RING)), dma((2, RING)),
            dma((3,)), dma((3,)), dma((2,)), dma((2,)),
            dma((2, FLOWS, 4)), dma((2, FLOWS, 4)), dma((FLOWS,)), dma((FLOWS,)),
        ],
        compiler_params=pltpu.CompilerParams(
            collective_id=0, has_side_effects=True, vmem_limit_bytes=60 * 1024 * 1024
        ),
        cost_estimate=pl.CostEstimate(
            flops=3_000_000_000, bytes_accessed=4_000_000, transcendentals=1_100_000
        ),
    )(query, key, value, query_tangent, key_tangent, value_tangent, out_weight, block_mask, probe)

    def write(main_in, tangent_in, trace_in, main_out, tangent_out, trace_out):
        main_out[...] = main_in[...]
        tangent_out[...] = tangent_in[...]
        trace_out[...] = trace_in[...]

    main, tangent, trace = pl.pallas_call(
        write,
        out_shape=(
            jax.ShapeDtypeStruct((8, width), bf16),
            jax.ShapeDtypeStruct((8, width), bf16),
            jax.ShapeDtypeStruct((1, 8), f32),
        ),
        in_specs=[in_vmem] * 3,
        out_specs=[in_vmem] * 3,
    )(main, tangent, trace)
    return main, tangent, trace.reshape(8)


def solution(mesh):
    placed = (
        P("ctx", "head"),
        P("ctx", "head"),
        P("ctx", "head"),
        P("ctx", "head"),
        P("ctx", "head"),
        P("ctx", "head"),
        P("head", None),
        P(),
        P(("ctx", "head"), None),
    )
    return jax.shard_map(
        on_device,
        mesh=mesh,
        in_specs=placed,
        out_specs=(P(("ctx", "head"), None), P(("ctx", "head"), None), P(("ctx", "head"))),
        check_vma=False,
    )
```

time: 501 us -> 70.9 us (0.14)
  the two profiles are of different devices: /device:TPU:8 before, /device:TPU:16 now
where the time goes in v1:
time: 70.9 us; the launch traced here: 70.7 us
  Pallas kernels  70 us (99%)
    pallas_call x1, Pallas kernels, on_device(): pl.pallas_call(kernel, out_shape=(jax.ShapeDtypeStruct((8, width), bf16),...  68.5 us
    pallas_call x1, Pallas kernels, on_device(): pl.pallas_call(write, out_shape=(jax.ShapeDtypeStruct((8, width), bf16),...  1.53 us

profile of v1, /device:TPU:16, one launch (start us, length us, event | category | flops | bytes accessed | tf_op | source)
XLA Modules:
  0.0 70.7 jit_solution(15634976359483982789)
XLA Ops:
  0.6 68.5 %shard_map.112 = (bf16[8,4096]{1,0:T(8,128)(2,1)}, bf16[8,4096]{1,0:T(8,128)(2,1)}, f32[1,8]{1,0:T(1,128)}) custom-call(bf16[128,256]{1,0:T(8,128)(2,1)} %query.1, bf16[128,256]{1,0:T(8,128)(2,1)} %key.1, bf16[128,256]{1,0:T(8,128)(2,1)} %value.1, bf16[128,256]{1,0:T(8,128)(2,1)} %query_t.1, bf16[128,256]{1,0:T(8,128)(2,1)} %key_t.1, ...), custom_call_target="tpu_custom_call" | custom-call | flops 3000000000 | bytes 4000000 | tf_op jit(solution)/shard_map/pallas_call | solution.py:418
  69.1 1.5 %shard_map.113 = (bf16[8,4096]{1,0:T(8,128)(2,1)}, bf16[8,4096]{1,0:T(8,128)(2,1)}, f32[1,8]{1,0:T(1,128)}) custom-call(bf16[8,4096]{1,0:T(8,128)(2,1)} %get-tuple-element.9.main_in, bf16[8,4096]{1,0:T(8,128)(2,1)} %get-tuple-element.10.tangent_in, f32[1,8]{1,0:T(1,128)} %get-tuple-element.11.trace_in), custom_call_target="tpu_custom_call" | custom-call | tf_op jit(solution)/shard_map/pallas_call | solution.py:461

commit v2 on v1

--- a/solution.py
+++ b/solution.py
@@ -30,9 +30,9 @@
     query, key, value, query_t, key_t, value_t, weight, mask, probe,
     out_main, out_tan, out_trace,
     shards, queries, peak, acc_v, acc_t, sums, att, att_in, w_buf, probe_buf, part,
-    z_out, z_in, x_out, x_in,
+    z_out, z_in,
     swap_send, swap_recv, local_sem, load_sem, ring_send, ring_recv, share_send, share_recv,
-    att_send, att_recv, w_send, w_recv, z_send, z_recv, x_send, x_recv,
+    att_send, att_recv, w_send, w_recv, z_send, z_recv,
 ):
     ctx = lax.axis_index("ctx")
     head = lax.axis_index("head")
@@ -41,8 +41,7 @@
     z, xlo = head % RING, head // RING
     far = 1 - half
     width = weight.shape[1]
-    wide = width // 2
-    cols = wide // FLOWS
+    cols = width // FLOWS
 
     sibling = {"ctx": chip * 2 + 1 - core, "head": head}
     opposite = {"ctx": (far * RING + y) * 2 + core, "head": head}
@@ -120,23 +119,33 @@
             message(d, 0, 0, e).start()
     share(0, 0).start()
 
-    my_cols = pl.ds(pl.multiple_of(xlo * wide, wide), wide)
-    its_cols = pl.ds(pl.multiple_of((1 - xlo) * wide, wide), wide)
     loads = [
-        pltpu.make_async_copy(weight.at[at, my_cols], w_buf.at[i], load_sem.at[i])
+        pltpu.make_async_copy(weight.at[at], w_buf.at[i], load_sem.at[i])
         for i, at in enumerate([mine, theirs])
     ] + [pltpu.make_async_copy(probe, probe_buf, load_sem.at[2])]
     for copy in loads:
         copy.start()
     turn = (core + half) % 2
-    w_fetch = remote(
-        weight.at[pl.ds(pl.multiple_of(core * HD, HD), HD), its_cols], w_buf.at[2 + turn],
-        w_send.at[0], w_recv.at[0], x_next,
-    )
+    w_rows = pl.ds(pl.multiple_of(core * HD, HD), HD)
+    halves = [pl.ds(0, width // 2), pl.ds(width // 2, width // 2)]
+    w_fetch = [
+        remote(
+            weight.at[w_rows, halves[i]], w_buf.at[2 + slot, :, halves[i]],
+            w_send.at[i], w_recv.at[i], device,
+        )
+        for i, (slot, device) in enumerate([(turn, x_next), (1 - turn, fourth)])
+    ]
+    w_landing = [
+        remote(
+            weight.at[w_rows, halves[i]], w_buf.at[2 + turn, :, halves[i]],
+            w_send.at[i], w_recv.at[i], device,
+        )
+        for i, device in enumerate([x_next, fourth])
+    ]
 
     def w_share(arriving=False):
         ref = w_buf.at[2 + (1 - turn if arriving else turn)]
-        return remote(ref, ref, w_send.at[1], w_recv.at[1], sibling)
+        return remote(ref, ref, w_send.at[2], w_recv.at[2], sibling)
 
     peak[...] = jnp.full(peak.shape, MASKED, jnp.float32)
     sums[...] = jnp.zeros(sums.shape, jnp.float32)
@@ -198,7 +207,8 @@
             message(d, 1, 0, e).start()
         if e == 1:
             share(1, 0).start()
-            w_fetch.start()
+            for copy in w_fetch:
+                copy.start()
 
     def send_rows():
         for copy in crossing[4:]:
@@ -209,7 +219,8 @@
             copy.wait_recv()
 
     def share_weight():
-        w_fetch.wait_recv()
+        for copy in w_landing:
+            copy.wait_recv()
         w_share().start()
 
     do = functools.partial
@@ -224,10 +235,10 @@
         ([do(ring, 1, 1, 0)], (1, 1)),
         ([do(ring, 1, 1, 1)], (0, -3)),
         ([do(last, 0)], (0, 3)),
-        ([share_weight], (1, -2)),
+        ([], (1, -2)),
         ([do(ring, 1, 2, 0)], (1, 2)),
         ([do(ring, 1, 2, 1)], (0, 4)),
-        ([], (1, -3)),
+        ([share_weight], (1, -3)),
         ([], (1, 3)),
         ([do(last, 1)], (1, 4)),
     ]
@@ -250,9 +261,13 @@
 
     lax.fori_loop(0, len(steps) - 1, step, 0)
 
+    own_rows = pl.ds(pl.multiple_of(xlo * BLOCK, BLOCK), BLOCK)
+    its_rows = pl.ds(pl.multiple_of((1 - xlo) * BLOCK, BLOCK), BLOCK)
     hand_back = [
-        remote(att.at[which], att_in.at[i], att_send.at[i], att_recv.at[i], device)
-        for i, (which, device) in enumerate([(far, opposite), (half, x_next), (far, fourth)])
+        remote(att.at[which, rows], att_in.at[i], att_send.at[i], att_recv.at[i], device)
+        for i, (which, rows, device) in enumerate(
+            [(far, own_rows, opposite), (half, its_rows, x_next), (far, its_rows, fourth)]
+        )
     ]
 
     def attended(b):
@@ -263,8 +278,8 @@
             acc_t[at, HD:] * SCALE
         ) / total * main
         pieces = []
-        for zz in range(RING):
-            for xx in range(2):
+        for xx in range(2):
+            for zz in range(RING):
                 first = (xx * RING + zz) * 8
                 pieces += [main[first : first + 8], tangent[first : first + 8]]
         att[b] = jnp.concatenate(pieces, axis=0).astype(jnp.bfloat16)
@@ -293,19 +308,20 @@
         copy.wait_send()
     for copy in loads:
         copy.wait()
-    w_fetch.wait_send()
+    for copy in w_fetch:
+        copy.wait_send()
     w_share().wait_send()
     w_share(True).wait_recv()
 
     def project(f, begin):
         at = slice(f * cols, (f + 1) * cols)
-        rows_in = [att[half], att_in[1]] if begin else [att_in[0], att_in[2]]
+        rows_in = [att[half, own_rows, :], att_in[2]] if begin else [att_in[0], att_in[1]]
         lhs = jnp.concatenate(rows_in, axis=1)
-        heads = (0, 2) if begin else (1, 3)
+        heads = (0, 3) if begin else (1, 2)
         term = dot(lhs, jnp.concatenate([w_buf[i, :, at] for i in heads], axis=0))
         part[:, at] = term if begin else part[:, at] + term
 
-    chunk = 32
+    chunk = 16
 
     def z_message(d, f, s):
         rows = pl.ds(0, chunk if s < 3 else chunk + 16)
@@ -328,7 +344,7 @@
         z_out[d, f, s, :chunk, :] = high
         if s == 3:
             low = low.astype(jnp.float32)
-            z_out[d, f, s, chunk:, :] = jnp.concatenate([low[8:16], low[24:]], axis=0).astype(
+            z_out[d, f, s, chunk:, :] = jnp.concatenate([low[8:], low[8:]], axis=0).astype(
                 jnp.bfloat16
             )
         z_message(d, f, s).start()
@@ -337,11 +353,11 @@
         return 1 if f < FLOWS // 2 else 0
 
     order = [f + side for f in range(FLOWS // 2) for side in (0, FLOWS // 2)]
-    hand_back[1].wait()
+    hand_back[2].wait()
     for f in order:
         project(f, True)
     hand_back[0].wait()
-    hand_back[2].wait()
+    hand_back[1].wait()
     for f in order:
         project(f, False)
         send_sum(far_side(f), f, 0, False)
@@ -352,47 +368,22 @@
             if s < 3:
                 send_sum(1 - far_side(f), f, s + 1, True)
 
-    def x_message(f):
-        return remote(x_out.at[f], x_in.at[f], x_send.at[f], x_recv.at[f], x_next)
-
-    def settle(f, which):
-        own = pl.ds(pl.multiple_of(which * 16, 16), 16)
+    trace = jnp.zeros((8, HD), jnp.float32)
+    for f in order:
+        final = part[pl.ds(pl.multiple_of(z * chunk, chunk), chunk), f * cols : (f + 1) * cols]
+        low = jnp.zeros((8, cols), jnp.float32)
+        for d in range(2):
+            z_message(d, f, 3).wait_recv()
+            landed = z_in[d, f, 3].astype(jnp.float32)
+            final = final + landed[:chunk]
+            low = low + landed[chunk : chunk + 8]
+        tangent = final[8:] + low
         at = slice(f * cols, (f + 1) * cols)
-        low = z_in[0, f, 3, chunk:, :].astype(jnp.float32) + z_in[1, f, 3, chunk:, :].astype(jnp.float32)
-        low = jnp.where(which == 0, low[:8], low[8:])
-        return (
-            part[pl.ds(pl.multiple_of(z * chunk + which * 16, 16), 16), at]
-            + z_in[0, f, 3, own, :].astype(jnp.float32)
-            + z_in[1, f, 3, own, :].astype(jnp.float32)
-            + jnp.concatenate([jnp.zeros_like(low), low], axis=0)
-        )
-
-    for f in order:
-        for d in range(2):
-            z_message(d, f, 3).wait_recv()
-        high, low = split(settle(f, 1 - xlo))
-        low = low.astype(jnp.float32)[8:]
-        x_out[f, :16, :] = high
-        x_out[f, 16:, :] = jnp.concatenate([low, jnp.zeros_like(low)], axis=0).astype(jnp.bfloat16)
-        x_message(f).start()
-
-    def finish(main, tangent, side, f, trace):
-        at = pl.ds(pl.multiple_of(side * wide + f * cols, cols), cols)
-        out_main[:, at] = main.astype(jnp.bfloat16)
+        out_main[:, at] = final[:8].astype(jnp.bfloat16)
         out_tan[:, at] = tangent.astype(jnp.bfloat16)
         signed = (2 * probe_buf[:, at] - 1).astype(jnp.float32) * tangent
         for i in range(cols // HD):
             trace = trace + signed[:, i * HD : (i + 1) * HD]
-        return trace
-
-    trace = jnp.zeros((8, HD), jnp.float32)
-    for f in order:
-        final = settle(f, xlo)
-        trace = finish(final[:8], final[8:], xlo, f, trace)
-    for f in order:
-        x_message(f).wait_recv()
-        final = x_in[f].astype(jnp.float32)
-        trace = finish(final[:8], final[8:16] + final[16:24], 1 - xlo, f, trace)
     at_row = lax.broadcasted_iota(jnp.int32, (8, HD), 0) == lax.broadcasted_iota(jnp.int32, (8, HD), 1)
     sums_of = jnp.broadcast_to(jnp.sum(trace, axis=1, keepdims=True) / math.sqrt(width), (8, HD))
     out_trace[...] = jnp.sum(jnp.where(at_row, sums_of, 0.0), axis=0, keepdims=True)[:, :8]
@@ -401,16 +392,13 @@
         for f in range(FLOWS):
             for s in range(0 if d == far_side(f) else 1, 4):
                 z_message(d, f, s).wait_send()
-    for f in range(FLOWS):
-        x_message(f).wait_send()
 
 
 def on_device(
     query, key, value, query_tangent, key_tangent, value_tangent, out_weight, block_mask, probe
 ):
     width = out_weight.shape[1]
-    wide = width // 2
-    cols = wide // FLOWS
+    cols = width // FLOWS
     anywhere = pl.BlockSpec(memory_space=pl.ANY)
     in_vmem = pl.BlockSpec(memory_space=pltpu.VMEM)
     bf16, f32 = jnp.bfloat16, jnp.float32
@@ -432,18 +420,16 @@
             pltpu.VMEM((PAIR, PAIR), f32),
             pltpu.VMEM((PAIR, HD), f32),
             pltpu.VMEM((2, PAIR, HD), bf16),
-            pltpu.VMEM((3, PAIR, HD), bf16),
-            pltpu.VMEM((4, HD, wide), bf16),
+            pltpu.VMEM((3, BLOCK, HD), bf16),
+            pltpu.VMEM((4, HD, width), bf16),
             pltpu.VMEM((8, width), jnp.int32),
-            pltpu.VMEM((PAIR, wide), f32),
-            pltpu.VMEM((2, FLOWS, 4, 48, cols), bf16),
-            pltpu.VMEM((2, FLOWS, 4, 48, cols), bf16),
-            pltpu.VMEM((FLOWS, 32, cols), bf16),
-            pltpu.VMEM((FLOWS, 32, cols), bf16),
+            pltpu.VMEM((BLOCK, width), f32),
+            pltpu.VMEM((2, FLOWS, 4, 32, cols), bf16),
+            pltpu.VMEM((2, FLOWS, 4, 32, cols), bf16),
             dma((6,)), dma((6,)), dma((6,)), dma((3,)),
             dma((2, 2, 4, 2)), dma((2, 2, 4, 2)), dma((2, RING)), dma((2, RING)),
-            dma((3,)), dma((3,)), dma((2,)), dma((2,)),
-            dma((2, FLOWS, 4)), dma((2, FLOWS, 4)), dma((FLOWS,)), dma((FLOWS,)),
+            dma((3,)), dma((3,)), dma((3,)), dma((3,)),
+            dma((2, FLOWS, 4)), dma((2, FLOWS, 4)),
         ],
         compiler_params=pltpu.CompilerParams(
             collective_id=0, has_side_effects=True, vmem_limit_bytes=60 * 1024 * 1024

time: 70.9 us -> 67.7 us (0.955)
  Pallas kernels: 70 us -> 66.6 us
    pallas_call x1, Pallas kernels: 68.5 us -> 65.1 us  [on_device(): pl.pallas_call(kernel, out_shape=(jax.ShapeDtypeStruct((8, width), bf16),...]
where the time goes in v2:
time: 67.7 us; the launch traced here: 67.3 us
  Pallas kernels  66.6 us (98%)
    pallas_call x1, Pallas kernels, on_device(): pl.pallas_call(kernel, out_shape=(jax.ShapeDtypeStruct((8, width), bf16),...  65.1 us
    pallas_call x1, Pallas kernels, on_device(): pl.pallas_call(write, out_shape=(jax.ShapeDtypeStruct((8, width), bf16),...  1.53 us

profile of v2, /device:TPU:16, one launch (start us, length us, event | category | flops | bytes accessed | tf_op | source)
XLA Modules:
  0.0 67.3 jit_solution(1568257228122319570)
XLA Ops:
  0.6 65.1 %shard_map.112 = (bf16[8,4096]{1,0:T(8,128)(2,1)}, bf16[8,4096]{1,0:T(8,128)(2,1)}, f32[1,8]{1,0:T(1,128)}) custom-call(bf16[128,256]{1,0:T(8,128)(2,1)} %query.1, bf16[128,256]{1,0:T(8,128)(2,1)} %key.1, bf16[128,256]{1,0:T(8,128)(2,1)} %value.1, bf16[128,256]{1,0:T(8,128)(2,1)} %query_t.1, bf16[128,256]{1,0:T(8,128)(2,1)} %key_t.1, ...), custom_call_target="tpu_custom_call" | custom-call | flops 3000000000 | bytes 4000000 | tf_op jit(solution)/shard_map/pallas_call | solution.py:406
  65.7 1.5 %shard_map.113 = (bf16[8,4096]{1,0:T(8,128)(2,1)}, bf16[8,4096]{1,0:T(8,128)(2,1)}, f32[1,8]{1,0:T(1,128)}) custom-call(bf16[8,4096]{1,0:T(8,128)(2,1)} %get-tuple-element.9.main_in, bf16[8,4096]{1,0:T(8,128)(2,1)} %get-tuple-element.10.tangent_in, f32[1,8]{1,0:T(1,128)} %get-tuple-element.11.trace_in), custom_call_target="tpu_custom_call" | custom-call | tf_op jit(solution)/shard_map/pallas_call | solution.py:447

commit v3 on v2

--- a/solution.py
+++ b/solution.py
@@ -225,19 +225,23 @@
 
     do = functools.partial
     steps = [
-        ([do(ring, 0, 0, 0), send_rows, do(ring, 0, 0, 1), do(cross, 0), do(cross, 1), rows_of_opposite], (0, 0)),
-        ([do(ring, 0, 1, 0)], (1, 0)),
-        ([do(ring, 0, 1, 1)], (0, -1)),
-        ([do(ring, 1, 0, 0)], (0, 1)),
-        ([do(ring, 1, 0, 1)], (0, -2)),
-        ([do(ring, 0, 2, 0)], (0, 2)),
-        ([do(ring, 0, 2, 1)], (1, -1)),
-        ([do(ring, 1, 1, 0)], (1, 1)),
-        ([do(ring, 1, 1, 1)], (0, -3)),
-        ([do(last, 0)], (0, 3)),
-        ([], (1, -2)),
-        ([do(ring, 1, 2, 0)], (1, 2)),
-        ([do(ring, 1, 2, 1)], (0, 4)),
+        (
+            [do(ring, 0, 0, 0), send_rows, do(ring, 0, 0, 1), do(cross, 0), do(cross, 1)]
+            + [do(ring, 0, 1, 0), rows_of_opposite],
+            (0, 0),
+        ),
+        ([do(ring, 0, 1, 1)], (1, 0)),
+        ([do(ring, 1, 0, 0)], (0, -1)),
+        ([do(ring, 1, 0, 1)], (0, 1)),
+        ([do(ring, 0, 2, 0)], (0, -2)),
+        ([do(ring, 0, 2, 1)], (0, 2)),
+        ([do(ring, 1, 1, 0)], (1, -1)),
+        ([do(ring, 1, 1, 1)], (1, 1)),
+        ([do(last, 0)], (0, -3)),
+        ([], (0, 3)),
+        ([do(ring, 1, 2, 0)], (1, -2)),
+        ([do(ring, 1, 2, 1)], (1, 2)),
+        ([], (0, 4)),
         ([share_weight], (1, -3)),
         ([], (1, 3)),
         ([do(last, 1)], (1, 4)),
@@ -324,10 +328,10 @@
     chunk = 16
 
     def z_message(d, f, s):
-        rows = pl.ds(0, chunk if s < 3 else chunk + 16)
+        at = pl.ds(0, cols if s < 3 else cols + cols // 2)
         return remote(
-            z_out.at[d, f, s, rows], z_in.at[d, f, s, rows], z_send.at[d, f, s], z_recv.at[d, f, s],
-            z_next[d],
+            z_out.at[d, f, s, :, at], z_in.at[d, f, s, :, at], z_send.at[d, f, s],
+            z_recv.at[d, f, s], z_next[d],
         )
 
     def send_sum(d, f, s, has_input):
@@ -339,14 +343,14 @@
             pl.ds(pl.multiple_of(target * chunk, chunk), chunk), f * cols : (f + 1) * cols
         ]
         if has_input:
-            summed = summed + z_in[d, f, s - 1, :chunk, :].astype(jnp.float32)
+            summed = summed + z_in[d, f, s - 1, :, :cols].astype(jnp.float32)
         high, low = split(summed)
-        z_out[d, f, s, :chunk, :] = high
+        z_out[d, f, s, :, :cols] = high
         if s == 3:
-            low = low.astype(jnp.float32)
-            z_out[d, f, s, chunk:, :] = jnp.concatenate([low[8:], low[8:]], axis=0).astype(
-                jnp.bfloat16
-            )
+            low = low.astype(jnp.float32)[8:]
+            z_out[d, f, s, :, cols:] = jnp.concatenate(
+                [low[:, : cols // 2], low[:, cols // 2 :]], axis=0
+            ).astype(jnp.bfloat16)
         z_message(d, f, s).start()
 
     def far_side(f):
@@ -375,8 +379,8 @@
         for d in range(2):
             z_message(d, f, 3).wait_recv()
             landed = z_in[d, f, 3].astype(jnp.float32)
-            final = final + landed[:chunk]
-            low = low + landed[chunk : chunk + 8]
+            final = final + landed[:, :cols]
+            low = low + jnp.concatenate([landed[:8, cols:], landed[8:, cols:]], axis=1)
         tangent = final[8:] + low
         at = slice(f * cols, (f + 1) * cols)
         out_main[:, at] = final[:8].astype(jnp.bfloat16)
@@ -424,8 +428,8 @@
             pltpu.VMEM((4, HD, width), bf16),
             pltpu.VMEM((8, width), jnp.int32),
             pltpu.VMEM((BLOCK, width), f32),
-            pltpu.VMEM((2, FLOWS, 4, 32, cols), bf16),
-            pltpu.VMEM((2, FLOWS, 4, 32, cols), bf16),
+            pltpu.VMEM((2, FLOWS, 4, 16, cols + cols // 2), bf16),
+            pltpu.VMEM((2, FLOWS, 4, 16, cols + cols // 2), bf16),
             dma((6,)), dma((6,)), dma((6,)), dma((3,)),
             dma((2, 2, 4, 2)), dma((2, 2, 4, 2)), dma((2, RING)), dma((2, RING)),
             dma((3,)), dma((3,)), dma((3,)), dma((3,)),

time: 67.7 us -> 66.2 us (0.978)
  Pallas kernels: 66.6 us -> 65.3 us
    pallas_call x1, Pallas kernels: 65.1 us -> 63.8 us  [on_device(): pl.pallas_call(kernel, out_shape=(jax.ShapeDtypeStruct((8, width), bf16),...]
where the time goes in v3:
time: 66.2 us; the launch traced here: 66 us
  Pallas kernels  65.3 us (99%)
    pallas_call x1, Pallas kernels, on_device(): pl.pallas_call(kernel, out_shape=(jax.ShapeDtypeStruct((8, width), bf16),...  63.8 us
    pallas_call x1, Pallas kernels, on_device(): pl.pallas_call(write, out_shape=(jax.ShapeDtypeStruct((8, width), bf16),...  1.53 us

profile of v3, /device:TPU:16, one launch (start us, length us, event | category | flops | bytes accessed | tf_op | source)
XLA Modules:
  0.0 66.0 jit_solution(10348389613432601651)
XLA Ops:
  0.6 63.8 %shard_map.112 = (bf16[8,4096]{1,0:T(8,128)(2,1)}, bf16[8,4096]{1,0:T(8,128)(2,1)}, f32[1,8]{1,0:T(1,128)}) custom-call(bf16[128,256]{1,0:T(8,128)(2,1)} %query.1, bf16[128,256]{1,0:T(8,128)(2,1)} %key.1, bf16[128,256]{1,0:T(8,128)(2,1)} %value.1, bf16[128,256]{1,0:T(8,128)(2,1)} %query_t.1, bf16[128,256]{1,0:T(8,128)(2,1)} %key_t.1, ...), custom_call_target="tpu_custom_call" | custom-call | flops 3000000000 | bytes 4000000 | tf_op jit(solution)/shard_map/pallas_call | solution.py:410
  64.5 1.5 %shard_map.113 = (bf16[8,4096]{1,0:T(8,128)(2,1)}, bf16[8,4096]{1,0:T(8,128)(2,1)}, f32[1,8]{1,0:T(1,128)}) custom-call(bf16[8,4096]{1,0:T(8,128)(2,1)} %get-tuple-element.9.main_in, bf16[8,4096]{1,0:T(8,128)(2,1)} %get-tuple-element.10.tangent_in, f32[1,8]{1,0:T(1,128)} %get-tuple-element.11.trace_in), custom_call_target="tpu_custom_call" | custom-call | tf_op jit(solution)/shard_map/pallas_call | solution.py:451
